TPU v7x, 32 devices: a whole 2x2x4 slice. The times are simulated.
32 devices in a mesh: energy: 8 (over y, x, core), mom: 4 (over z).
Axes of the slice: x: 2, y: 2, z: 4, core: 2. Of those that a mesh axis runs over, the one named last changes fastest.
Arguments:
- green_ret: bfloat16 [8, 4, 12, 3, 2, 128, 128], P('energy', 'mom'), may hold values from -0.5 to 0.5
- sigma_in: bfloat16 [8, 4, 12, 2, 128, 128], P('energy', 'mom'), may hold values from -6 to 6
- coupling: bfloat16 [4, 128, 128], replicated, may hold values from -0.5 to 0.5
- pattern: int32 [12], replicated, may hold values from 0 to 3
- neighbours: int32 [4, 3], P('mom'), may hold values from -1 to 1
- offsets: int32 [32], replicated, may hold values from -8 to 8, as said below
- tap_weight: float32 [32], replicated, may hold values from 0.005 to 0.04
Outputs:
- self_energy: bfloat16 [8, 4, 2, 1536, 128], P(None, 'mom', None, 'energy')
Inputs may be any that keep to these rules, and one draw needn't show every extreme that they name: `offsets`: both ends of the range are taken by some tap.
All inputs are finite; a program needn't handle non-finite values.
Results may differ from a plain program's by a relative error of at most 0.0081.
Values may be sent and summed in bfloat16 or wider, within the bound.
A program may use at most 64 MiB of HBM per device.

v0:
```python
import jax
import jax.numpy as jnp
from jax import lax
from jax.sharding import PartitionSpec as P


def shifted(value, axis, steps):
    count = lax.axis_size(axis)
    pairs = [(source, (source + steps) % count) for source in range(count)]
    return lax.ppermute(value, axis, pairs)


def batched(left, right):
    return jnp.einsum("sab,sbc->sac", left, right, preferred_element_type=jnp.float32)


def batched_adjoint(left, right):
    return jnp.einsum("sab,scb->sac", left, right, preferred_element_type=jnp.float32)


def slab_lesser(green, padded, slab_coupling, first, last):
    orbitals = green.shape[-1]
    count = last - first
    couple = slab_coupling[first:last]
    total_real = jnp.zeros((count, orbitals, orbitals), jnp.float32)
    total_imag = jnp.zeros((count, orbitals, orbitals), jnp.float32)
    for term in range(3):
        near = padded[first + term : last + term]
        block = green[first:last, term]
        coupled_real = batched(couple, block[:, 0]).astype(jnp.bfloat16)
        coupled_imag = batched(couple, block[:, 1]).astype(jnp.bfloat16)
        left_real = (batched(coupled_real, near[:, 0]) - batched(coupled_imag, near[:, 1])).astype(
            jnp.bfloat16
        )
        left_imag = (batched(coupled_real, near[:, 1]) + batched(coupled_imag, near[:, 0])).astype(
            jnp.bfloat16
        )
        total_real = (
            total_real
            + batched_adjoint(left_real, coupled_real)
            + batched_adjoint(left_imag, coupled_imag)
        )
        total_imag = (
            total_imag
            + batched_adjoint(left_imag, coupled_real)
            - batched_adjoint(left_real, coupled_imag)
        )
    rows = count * orbitals
    return jnp.stack(
        [total_real.reshape(rows, orbitals), total_imag.reshape(rows, orbitals)]
    ).astype(jnp.bfloat16)


def shards(green_ret, sigma_in, coupling, pattern, neighbours, offsets, tap_weight):
    e_local = green_ret.shape[0]
    energies = e_local * lax.axis_size("energy")
    slabs = green_ret.shape[2]
    half = slabs // 2
    kinds = coupling.shape[0]
    onehot = (pattern[:, None] == jnp.arange(kinds, dtype=jnp.int32)[None, :]).astype(jnp.bfloat16)
    slab_coupling = jnp.dot(onehot, coupling.reshape(kinds, -1), preferred_element_type=jnp.float32)
    slab_coupling = slab_coupling.astype(jnp.bfloat16).reshape(
        slabs, coupling.shape[1], coupling.shape[2]
    )
    weights = [jnp.sum((neighbours[0] == side).astype(jnp.float32)) for side in (-1, 0, 1)]
    index = jnp.arange(energies, dtype=jnp.int32)
    hit = index[None, :, None] == index[:, None, None] - offsets[None, None, :]
    banded = jnp.sum(
        jnp.where(hit, tap_weight[None, None, :], jnp.zeros((), jnp.float32)), axis=2
    ).astype(jnp.bfloat16)
    green = green_ret[0, 0]
    padded = jnp.pad(sigma_in[0, 0], ((1, 1), (0, 0), (0, 0), (0, 0)))
    pieces = []
    for first in (0, half):
        piece = slab_lesser(green, padded, slab_coupling, first, first + half)
        below = shifted(piece, "mom", 1)
        above = shifted(piece, "mom", -1)
        total = weights[0] * below.astype(jnp.float32) + weights[1] * piece.astype(jnp.float32)
        pieces.append((total + weights[2] * above.astype(jnp.float32)).astype(jnp.bfloat16))
    mixed_parts = [jnp.concatenate(pieces, axis=1)]
    mixed = jnp.stack(mixed_parts)
    result = jnp.einsum(
        "ef,fcrk->ecrk",
        banded,
        lax.all_to_all(mixed, "energy", split_axis=2, concat_axis=0, tiled=True),
        preferred_element_type=jnp.float32,
    ).astype(jnp.bfloat16)
    return result[:, None]


def solution(mesh):
    return jax.shard_map(
        shards,
        mesh=mesh,
        in_specs=(
            P("energy", "mom", None, None, None, None, None),
            P("energy", "mom", None, None, None, None),
            P(),
            P(),
            P("mom", None),
            P(),
            P(),
        ),
        out_specs=P(None, "mom", None, "energy", None),
        check_vma=False,
    )
```

profile of v0, /device:TPU:0, one launch (start us, length us, event | category | flops | bytes accessed | tf_op | source)
XLA Modules:
  0.0 78.1 jit_solution(17315510375331789014)
XLA Ops:
  0.0 1.8 %copy.124 = bf16[1,1,12,3,2,128,128]{6,5,2,4,3,1,0:T(8,128)(2,1)S(1)} copy(bf16[1,1,12,3,2,128,128]{6,5,4,3,2,1,0:T(8,128)(2,1)} %param.7) | data formatting | bytes 4718592 | tf_op args[0]
  1.8 0.3 slice_bitcast_fusion.6
  2.1 0.6 copy-done.1
  2.7 0.3 convolution_convert_fusion
  8.2 0.3 convolution_add_fusion.8
  9.0 0.3 convolution_add_fusion.7
  9.2 0.3 convolution_add_fusion.5
  9.5 0.3 convolution_add_fusion
  9.8 0.3 fusion.16
  10.3 0.3 fusion.15
  10.6 5.1 %collective-permute-start.3 = (bf16[2,768,128]{2,1,0:T(8,128)(2,1)S(1)}, bf16[2,768,128]{2,1,0:T(8,128)(2,1)S(1)}, u32[]{:S(2)}, u32[]{:S(2)}) collective-permute-start(bf16[2,768,128]{2,1,0:T(8,128)(2,1)S(1)} %pad_maximum_fusion.1), channel_id=1, source_target_pairs={{0,3},{1,0},{2,1},{3,2},{4,7},{5,4},{6,5},{7,6},{8,11},{9,8},{10,9... | collective-permute-start | bytes 1179656 | tf_op jit(solution)/shard_map/ppermute | solution.py:10
  21.5 0.3 convolution_add_fusion.10
  22.7 3.9 %collective-permute-start.1 = (bf16[2,768,128]{2,1,0:T(8,128)(2,1)S(1)}, bf16[2,768,128]{2,1,0:T(8,128)(2,1)S(1)}, u32[]{:S(2)}, u32[]{:S(2)}) collective-permute-start(bf16[2,768,128]{2,1,0:T(8,128)(2,1)S(1)} %pad_maximum_fusion), channel_id=1, source_target_pairs={{0,3},{1,0},{2,1},{3,2},{4,7},{5,4},{6,5},{7,6},{8,11},{9,8},{10,9... | collective-permute-start | bytes 1179656 | tf_op jit(solution)/shard_map/ppermute | solution.py:10
  26.6 0.6 fusion.60
  27.2 7.4 %collective-permute-done.2 = bf16[2,768,128]{2,1,0:T(8,128)(2,1)S(1)} collective-permute-done((bf16[2,768,128]{2,1,0:T(8,128)(2,1)S(1)}, bf16[2,768,128]{2,1,0:T(8,128)(2,1)S(1)}, u32[]{:S(2)}, u32[]{:S(2)}) %collective-permute-start.2) | collective-permute-done | bytes 393248 | tf_op jit(solution)/shard_map/ppermute | solution.py:10
  34.6 2.1 %add_convert_fusion = bf16[2,768,128]{2,1,0:T(8,128)(2,1)S(1)} fusion(bf16[2,768,128]{2,1,0:T(8,128)(2,1)S(1)} %collective-permute-done.3, bf16[2,768,128]{2,1,0:T(8,128)(2,1)S(1)} %collective-permute-done.2, f32[]{:T(128)} %get-tuple-element.6, f32[]{:T(128)} %get-tuple-element.7, f32[]{:T(128)} %get-tuple-element.5, bf16[1,768,128]{2,1,0:T(8,128)(2,1)S(1)} %bitcast.254, ...), kind=kLoop, calls=%fused_computation.71 | loop fusion | flops 1966080 | bytes 1572876 | tf_op jit(solution)/shard_map/convert_element_type | solution.py:79
  36.7 5.5 %collective-permute-done.1 = bf16[2,768,128]{2,1,0:T(8,128)(2,1)S(1)} collective-permute-done((bf16[2,768,128]{2,1,0:T(8,128)(2,1)S(1)}, bf16[2,768,128]{2,1,0:T(8,128)(2,1)S(1)}, u32[]{:S(2)}, u32[]{:S(2)}) %collective-permute-start.1) | collective-permute-done | bytes 393248 | tf_op jit(solution)/shard_map/ppermute | solution.py:10
  42.1 8.2 %collective-permute-done = bf16[2,768,128]{2,1,0:T(8,128)(2,1)S(1)} collective-permute-done((bf16[2,768,128]{2,1,0:T(8,128)(2,1)S(1)}, bf16[2,768,128]{2,1,0:T(8,128)(2,1)S(1)}, u32[]{:S(2)}, u32[]{:S(2)}) %collective-permute-start) | collective-permute-done | bytes 393248 | tf_op jit(solution)/shard_map/ppermute | solution.py:10
  50.3 2.1 %add_convert_fusion.1 = bf16[2,768,128]{2,1,0:T(8,128)(2,1)S(1)} fusion(bf16[2,768,128]{2,1,0:T(8,128)(2,1)S(1)} %collective-permute-done.1, bf16[2,768,128]{2,1,0:T(8,128)(2,1)S(1)} %collective-permute-done, f32[]{:T(128)} %get-tuple-element.6, f32[]{:T(128)} %get-tuple-element.7, f32[]{:T(128)} %get-tuple-element.5, bf16[1,768,128]{2,1,0:T(8,128)(2,1)S(1)} %bitcast.258, ...), kind=kLoop, calls=%fused_computation.72 | loop fusion | flops 1966080 | bytes 1572876 | tf_op jit(solution)/shard_map/convert_element_type | solution.py:79
  52.5 7.3 %copy.55 = bf16[1,2,1536,128]{3,1,0,2:T(2,128)(2,1)} copy(bf16[1,2,1536,128]{3,2,1,0:T(8,128)(2,1)S(1)} %maximum_bitcast_fusion) | data formatting | bytes 1572864 | tf_op jit(solution)/shard_map/stack | solution.py:81
  59.7 3.7 %all-to-all-start = ((bf16[1,2,1536,128]{3,1,0,2:T(2,128)(2,1)}), bf16[1,2,1536,128]{3,1,0,2:T(2,128)(2,1)S(1)}, u32[]{:S(2)}, u32[]{:S(2)}) async-start(bf16[1,2,1536,128]{3,1,0,2:T(2,128)(2,1)} %copy.55), calls=%async_computation | async-start | bytes 1572864 | tf_op jit(solution)/shard_map/all_to_all | solution.py:85
  63.6 12.5 %all-to-all-done = bf16[1,2,1536,128]{3,1,0,2:T(2,128)(2,1)S(1)} async-done(((bf16[1,2,1536,128]{3,1,0,2:T(2,128)(2,1)}), bf16[1,2,1536,128]{3,1,0,2:T(2,128)(2,1)S(1)}, u32[]{:S(2)}, u32[]{:S(2)}) %all-to-all-start) | async-done | bytes 786464 | tf_op jit(solution)/shard_map/all_to_all | solution.py:85
  76.0 1.0 %fusion = bf16[8,1,2,192,128]{4,0,3,2,1:T(8,128)(2,1)S(1)} fusion(bf16[1,2,8,192,128]{4,1,3,2,0:T(2,128)(2,1)S(1)} %bitcast.252, bf16[8,8]{1,0:T(8,128)(2,1)S(1)} %select_reduce_fusion), kind=kOutput, calls=%fused_computation.3 | convolution fusion | flops 6684672 | bytes 1572992 | tf_op jit(solution)/shard_map/ef,fcrk->ecrk/dot_general | solution.py:82
  77.0 1.1 %copy.58 = bf16[8,1,2,192,128]{4,3,2,1,0:T(8,128)(2,1)} copy(bf16[8,1,2,192,128]{4,0,3,2,1:T(8,128)(2,1)S(1)} %fusion) | data formatting | bytes 1572864 | tf_op jit(solution)/shard_map/broadcast_in_dim | solution.py:88
  (75 shorter events, 12.4 us)
Async XLA Ops:
  1.8 0.9 %copy-start.1 = (bf16[4,128,128]{2,1,0:T(8,128)(2,1)S(1)}, bf16[4,128,128]{2,1,0:T(8,128)(2,1)}, u32[]{:S(2)}) copy-start(bf16[4,128,128]{2,1,0:T(8,128)(2,1)} %param.9) | copy-start | bytes 393220
  1.8 0.9 %copy-start.5 = (s32[12]{0:T(128)S(1)}, s32[12]{0:T(128)}, u32[]{:S(2)}) copy-start(s32[12]{0:T(128)} %param.10) | copy-start | bytes 148
  3.4 1.1 %copy-start = (bf16[1,1,12,2,128,128]{5,4,3,2,1,0:T(8,128)(2,1)S(1)}, bf16[1,1,12,2,128,128]{5,4,3,2,1,0:T(8,128)(2,1)}, u32[]{:S(2)}) copy-start(bf16[1,1,12,2,128,128]{5,4,3,2,1,0:T(8,128)(2,1)} %param.8) | copy-start | bytes 2359300
  10.6 16.5 %collective-permute-start.3 = (bf16[2,768,128]{2,1,0:T(8,128)(2,1)S(1)}, bf16[2,768,128]{2,1,0:T(8,128)(2,1)S(1)}, u32[]{:S(2)}, u32[]{:S(2)}) collective-permute-start(bf16[2,768,128]{2,1,0:T(8,128)(2,1)S(1)} %pad_maximum_fusion.1), channel_id=1, source_target_pairs={{0,3},{1,0},{2,1},{3,2},{4,7},{5,4},{6,5},{7,6},{8,11},{9,8},{10,9... | collective-permute-start | bytes 1179656 | tf_op jit(solution)/shard_map/ppermute | solution.py:10
  15.7 18.9 %collective-permute-start.2 = (bf16[2,768,128]{2,1,0:T(8,128)(2,1)S(1)}, bf16[2,768,128]{2,1,0:T(8,128)(2,1)S(1)}, u32[]{:S(2)}, u32[]{:S(2)}) collective-permute-start(bf16[2,768,128]{2,1,0:T(8,128)(2,1)S(1)} %pad_maximum_fusion.1), channel_id=1, source_target_pairs={{0,1},{1,2},{2,3},{3,0},{4,5},{5,6},{6,7},{7,4},{8,9},{9,10},{10,1... | collective-permute-start | bytes 1179656 | tf_op jit(solution)/shard_map/ppermute | solution.py:10
  22.1 4.5 %copy-start.3 = (s32[1,3]{1,0:T(1,128)S(1)}, s32[1,3]{1,0:T(1,128)}, u32[]{:S(2)}) copy-start(s32[1,3]{1,0:T(1,128)} %param.11) | copy-start | bytes 40
  22.7 19.5 %collective-permute-start.1 = (bf16[2,768,128]{2,1,0:T(8,128)(2,1)S(1)}, bf16[2,768,128]{2,1,0:T(8,128)(2,1)S(1)}, u32[]{:S(2)}, u32[]{:S(2)}) collective-permute-start(bf16[2,768,128]{2,1,0:T(8,128)(2,1)S(1)} %pad_maximum_fusion), channel_id=1, source_target_pairs={{0,3},{1,0},{2,1},{3,2},{4,7},{5,4},{6,5},{7,6},{8,11},{9,8},{10,9... | collective-permute-start | bytes 1179656 | tf_op jit(solution)/shard_map/ppermute | solution.py:10
  26.5 23.8 %collective-permute-start = (bf16[2,768,128]{2,1,0:T(8,128)(2,1)S(1)}, bf16[2,768,128]{2,1,0:T(8,128)(2,1)S(1)}, u32[]{:S(2)}, u32[]{:S(2)}) collective-permute-start(bf16[2,768,128]{2,1,0:T(8,128)(2,1)S(1)} %pad_maximum_fusion), channel_id=1, source_target_pairs={{0,1},{1,2},{2,3},{3,0},{4,5},{5,6},{6,7},{7,4},{8,9},{9,10},{10,1... | collective-permute-start | bytes 1179656 | tf_op jit(solution)/shard_map/ppermute | solution.py:10
  52.4 11.0 %copy-start.2 = (s32[32]{0:T(128)S(1)}, s32[32]{0:T(128)}, u32[]{:S(2)}) copy-start(s32[32]{0:T(128)} %param.12) | copy-start | bytes 388
  52.5 11.0 %copy-start.4 = (f32[32]{0:T(128)S(1)}, f32[32]{0:T(128)}, u32[]{:S(2)}) copy-start(f32[32]{0:T(128)} %param.13) | copy-start | bytes 388
  59.7 16.3 %all-to-all-start = ((bf16[1,2,1536,128]{3,1,0,2:T(2,128)(2,1)}), bf16[1,2,1536,128]{3,1,0,2:T(2,128)(2,1)S(1)}, u32[]{:S(2)}, u32[]{:S(2)}) async-start(bf16[1,2,1536,128]{3,1,0,2:T(2,128)(2,1)} %copy.55), calls=%async_computation | async-start | bytes 1572864 | tf_op jit(solution)/shard_map/all_to_all | solution.py:85
where the time goes:
time: 78.4 us; the launch traced here: 78.1 us
  waiting for transfers between devices  33.6 us (43%)
  matrix products  14.8 us (19%)
  starting transfers between devices  12.7 us (16%)
  local copies, waits for them, and re-layouts  11.6 us (15%)
  other arithmetic  4.95 us (6%)
    ppermute x4, waiting for transfers between devices, shifted(): return lax.ppermute(value, axis, pairs)  21.1 us
    all_to_all x1, waiting for transfers between devices, shards(): lax.all_to_all(mixed, 'energy', split_axis=2, concat_axis=0, tiled=True)  12.5 us
    ppermute x4, starting transfers between devices, shifted(): return lax.ppermute(value, axis, pairs)  8.98 us
    another operation x1, local copies, waits for them, and re-layouts, shards(): mixed = jnp.stack(mixed_parts)  7.26 us
    dot_general x36, matrix products, batched(): jnp.einsum('sab,sbc->sac', left, right, preferred_element_type=jnp.float32)  7.14 us
    dot_general x24, matrix products, batched_adjoint(): jnp.einsum('sab,scb->sac', left, right, preferred_element_type=jnp.float32)  6.33 us
    convert_element_type x2, other arithmetic, shards(): (total + weights[2] * above.astype(jnp.float32)).astype(jnp.bfloat16)  4.11 us
    all_to_all x1, starting transfers between devices, shards(): lax.all_to_all(mixed, 'energy', split_axis=2, concat_axis=0, tiled=True)  3.71 us
  transfers between devices with their start and end apart: 5, of which 4 were waited for; matrix products, arithmetic and copies ran while one was open for 12% of the time, Pallas kernels for 0%

commit v1 on v0

v1 whole, which is shorter than its diff:
```python
import functools
import math

import jax
import jax.numpy as jnp
from jax import lax
from jax.experimental import pallas as pl
from jax.experimental.pallas import tpu as pltpu
from jax.sharding import PartitionSpec as P

MESH = pl.DeviceIdType.MESH


def kernel(
    energies,
    momenta,
    green,
    sigma,
    coupling,
    pattern,
    neighbours,
    offsets,
    tap_weight,
    out,
    gbuf,
    sbuf,
    lesser,
    halo,
    mixed,
    gathered,
    table,
    gsem,
    ssem,
    zsend,
    zrecv,
    asend,
    arecv,
):
    slabs, _, _, orb, _ = gbuf.shape
    own_rows = gathered.shape[2]
    unit = math.gcd(orb, own_rows)
    per_slab = orb // unit
    per_owner = own_rows // unit
    me = lax.axis_index("energy")
    mom = lax.axis_index("mom")
    above = lax.rem(mom + 1, momenta)
    below = lax.rem(mom + momenta - 1, momenta)

    group = me // 2
    span = max(1, 2 * own_rows // orb)
    start = lax.rem(group * (2 * own_rows) // orb + span, slabs)

    def slab_at(step):
        return lax.rem(start + step, slabs)

    barrier = pltpu.get_barrier_semaphore()
    for to in (above, below):
        pl.semaphore_signal(barrier, inc=1, device_id={"mom": to}, device_id_type=MESH)
    for step in range(1, energies):
        to = lax.rem(me + step, energies)
        pl.semaphore_signal(barrier, inc=1, device_id={"energy": to}, device_id_type=MESH)

    sigma_copy = pltpu.make_async_copy(sigma.at[0, 0], sbuf.at[pl.ds(1, slabs)], ssem)
    sigma_copy.start()

    def green_copy(slab):
        return pltpu.make_async_copy(green.at[0, 0, slab], gbuf.at[slab], gsem.at[slab])

    @pl.loop(0, slabs)
    def _(step):
        green_copy(slab_at(step)).start()

    sbuf[0] = jnp.zeros(sbuf.shape[1:], sbuf.dtype)
    sbuf[slabs + 1] = jnp.zeros(sbuf.shape[1:], sbuf.dtype)
    sigma_copy.wait()

    def halo_copy(slab, side, to):
        return pltpu.make_async_remote_copy(
            src_ref=lesser.at[slab],
            dst_ref=halo.at[side, slab],
            send_sem=zsend.at[side, slab],
            recv_sem=zrecv.at[side, slab],
            device_id={"mom": to},
            device_id_type=MESH,
        )

    low = (mom < momenta // 2).astype(jnp.int32)
    first_to = jnp.where(low == 1, below, above)
    second_to = jnp.where(low == 1, above, below)

    @pl.loop(0, slabs)
    def _(step):
        slab = slab_at(step)
        green_copy(slab).wait()
        couple = coupling[pattern[slab]]
        total = jnp.zeros((orb, 2 * orb), jnp.float32)
        for term in range(3):
            block = jnp.concatenate([gbuf[slab, term, 0], gbuf[slab, term, 1]], axis=1)
            coupled = jnp.dot(couple, block, preferred_element_type=jnp.float32)
            coupled = coupled.astype(jnp.bfloat16)
            near_real = sbuf[slab + term, 0]
            near_imag = sbuf[slab + term, 1]
            near = jnp.concatenate(
                [
                    jnp.concatenate([near_real, near_imag], axis=1),
                    jnp.concatenate([-near_imag, near_real], axis=1),
                ],
                axis=0,
            )
            left = jnp.dot(coupled, near, preferred_element_type=jnp.float32)
            left = left.astype(jnp.bfloat16)
            turned = jnp.concatenate([-coupled[:, orb:], coupled[:, :orb]], axis=1)
            adjoint = jnp.concatenate([coupled, turned], axis=0)
            total = total + lax.dot_general(
                left, adjoint, (((1,), (1,)), ((), ())), preferred_element_type=jnp.float32
            )
        total = total.astype(jnp.bfloat16)
        lesser[slab, 0] = total[:, :orb]
        lesser[slab, 1] = total[:, orb:]

        @pl.when(step == 0)
        def _():
            pl.semaphore_wait(barrier, energies + 1)

        halo_copy(slab, low, first_to).start()
        halo_copy(slab, 1 - low, second_to).start()

    shift = lax.broadcasted_iota(jnp.int32, table.shape, 0) - (energies - 1)
    summed = jnp.zeros(table.shape, jnp.float32)
    for tap in range(offsets.shape[0]):
        summed = summed + jnp.where(shift == offsets[tap], tap_weight[tap], 0.0)
    table[...] = summed.astype(jnp.bfloat16).astype(jnp.float32)

    def count(side):
        total = jnp.float32(0.0)
        for entry in range(neighbours.shape[1]):
            total = total + jnp.where(neighbours[0, entry] == side, 1.0, 0.0)
        return total

    weights = [count(side) for side in (-1, 0, 1)]

    def mixed_copy(slab, part, to, source, place):
        return pltpu.make_async_remote_copy(
            src_ref=mixed.at[slab, :, pl.ds(part * unit, unit), :],
            dst_ref=gathered.at[source, :, pl.ds(place * unit, unit), :],
            send_sem=asend.at[slab, part],
            recv_sem=arecv.at[source, place],
            device_id={"energy": to},
            device_id_type=MESH,
        )

    @pl.loop(0, slabs)
    def _(step):
        slab = slab_at(step)
        halo_copy(slab, 0, above).wait_recv()
        halo_copy(slab, 1, below).wait_recv()
        for part in range(per_slab):
            rows = pl.ds(part * unit, unit)
            value = weights[0] * halo[0, slab, :, rows, :].astype(jnp.float32)
            value = value + weights[1] * lesser[slab, :, rows, :].astype(jnp.float32)
            value = value + weights[2] * halo[1, slab, :, rows, :].astype(jnp.float32)
            value = value.astype(jnp.bfloat16)
            piece = slab * per_slab + part
            owner = piece // per_owner
            place = lax.rem(piece, per_owner)

            @pl.when(owner == me)
            def _():
                gathered[me, :, pl.ds(pl.multiple_of(place * unit, unit), unit), :] = value

            @pl.when(owner != me)
            def _():
                mixed[slab, :, rows, :] = value
                mixed_copy(slab, part, owner, me, place).start()

    for place in range(per_owner):
        for step in range(1, energies):
            source = lax.rem(me + step, energies)
            mixed_copy(0, 0, source, source, place).wait_recv()

        block = 16
        blocks = unit // block

        @pl.loop(0, 2 * blocks)
        def _(index):
            part = index // blocks
            rows = pl.ds(
                pl.multiple_of(place * unit + lax.rem(index, blocks) * block, block), block
            )
            values = [gathered[f, part, rows, :].astype(jnp.float32) for f in range(energies)]
            for e in range(energies):
                total = None
                for f in range(energies):
                    term = table[pl.ds(e - f + energies - 1, 1), :] * values[f]
                    total = term if total is None else total + term
                out[e, 0, part, rows, :] = total.astype(jnp.bfloat16)

    @pl.loop(0, slabs)
    def _(slab):
        halo_copy(slab, 0, above).wait_send()
        halo_copy(slab, 1, below).wait_send()
        for part in range(per_slab):
            piece = slab * per_slab + part
            owner = piece // per_owner

            @pl.when(owner != me)
            def _():
                mixed_copy(slab, part, owner, me, lax.rem(piece, per_owner)).wait_send()


def shards(green_ret, sigma_in, coupling, pattern, neighbours, offsets, tap_weight):
    energies = lax.axis_size("energy")
    momenta = lax.axis_size("mom")
    slabs = green_ret.shape[2]
    orb = green_ret.shape[-1]
    own_rows = slabs * orb // energies
    unit = math.gcd(orb, own_rows)
    table_rows = -(-(2 * energies - 1) // 8) * 8
    any_space = pl.BlockSpec(memory_space=pl.ANY)
    vmem = pl.BlockSpec(memory_space=pltpu.VMEM)
    smem = pl.BlockSpec(memory_space=pltpu.SMEM)
    bf16 = jnp.bfloat16
    products = 30 * slabs * orb**3
    return pl.pallas_call(
        functools.partial(kernel, energies, momenta),
        out_shape=jax.ShapeDtypeStruct((energies, 1, 2, own_rows, orb), bf16),
        in_specs=[any_space, any_space, vmem, smem, smem, smem, smem],
        out_specs=vmem,
        scratch_shapes=[
            pltpu.VMEM((slabs, 3, 2, orb, orb), bf16),
            pltpu.VMEM((slabs + 2, 2, orb, orb), bf16),
            pltpu.VMEM((slabs, 2, orb, orb), bf16),
            pltpu.VMEM((2, slabs, 2, orb, orb), bf16),
            pltpu.VMEM((slabs, 2, orb, orb), bf16),
            pltpu.VMEM((energies, 2, own_rows, orb), bf16),
            pltpu.VMEM((table_rows, orb), jnp.float32),
            pltpu.SemaphoreType.DMA((slabs,)),
            pltpu.SemaphoreType.DMA,
            pltpu.SemaphoreType.DMA((2, slabs)),
            pltpu.SemaphoreType.DMA((2, slabs)),
            pltpu.SemaphoreType.DMA((slabs, orb // unit)),
            pltpu.SemaphoreType.DMA((energies, own_rows // unit)),
        ],
        compiler_params=pltpu.CompilerParams(
            collective_id=0, has_side_effects=True, vmem_limit_bytes=32 * 1024 * 1024
        ),
        cost_estimate=pl.CostEstimate(
            flops=2 * products, bytes_accessed=8 * slabs * orb * orb * 2, transcendentals=0
        ),
    )(green_ret, sigma_in, coupling, pattern, neighbours, offsets, tap_weight)


def solution(mesh):
    return jax.shard_map(
        shards,
        mesh=mesh,
        in_specs=(
            P("energy", "mom", None, None, None, None, None),
            P("energy", "mom", None, None, None, None),
            P(),
            P(),
            P("mom", None),
            P(),
            P(),
        ),
        out_specs=P(None, "mom", None, "energy", None),
        check_vma=False,
    )
```

time: 78.4 us -> 53.8 us (0.69)
  Pallas kernels: 0 us -> 46.1 us
  waiting for transfers between devices: 33.6 us -> 0 us
  matrix products: 14.8 us -> 0 us
  starting transfers between devices: 12.7 us -> 0 us
  other arithmetic: 4.95 us -> 0 us
  local copies, waits for them, and re-layouts: 11.6 us -> 7.2 us
    pallas_call x0 -> x1, Pallas kernels: none -> 46.1 us  [shards(): pl.pallas_call(functools.partial(kernel, energies, momenta), out_shape=ja...]
    ppermute x4 -> x0, waiting for transfers between devices: 21.1 us -> none  [shifted(): return lax.ppermute(value, axis, pairs)]
    dot_general x62 -> x0, matrix products: 14.8 us -> none  [the longest x36 7.14 us: batched(): jnp.einsum('sab,sbc->sac', left, right, preferred_element_type=jnp.float32)]
    all_to_all x1 -> x0, waiting for transfers between devices: 12.5 us -> none  [shards(): lax.all_to_all(mixed, 'energy', split_axis=2, concat_axis=0, tiled=True)]
    ppermute x4 -> x0, starting transfers between devices: 8.98 us -> none  [shifted(): return lax.ppermute(value, axis, pairs)]
    another operation x1 -> x0, local copies, waits for them, and re-layouts: 7.26 us -> none  [shards(): mixed = jnp.stack(mixed_parts)]
    unnamed x15, local copies, waits for them, and re-layouts: 2.72 us -> 7.2 us
    convert_element_type x2 -> x0, other arithmetic: 4.11 us -> none  [shards(): (total + weights[2] * above.astype(jnp.float32)).astype(jnp.bfloat16)]
  transfers between devices with their start and end apart: 5 -> 0, of which waited for: 4 -> 0; matrix products, arithmetic and copies ran while one was open for 12% -> 0% of each run, Pallas kernels for 0% -> 0%
where the time goes in v1:
time: 53.8 us; the launch traced here: 53.3 us
  Pallas kernels  46.1 us (86%)
  local copies, waits for them, and re-layouts  7.2 us (13%)
    pallas_call x1, Pallas kernels, shards(): pl.pallas_call(functools.partial(kernel, energies, momenta), out_shape=ja...  46.1 us
    unnamed x15, local copies, waits for them, and re-layouts  7.2 us

profile of v1, /device:TPU:0, one launch (start us, length us, event | category | flops | bytes accessed | tf_op | source)
XLA Modules:
  0.0 53.3 jit_solution(1565573141537035091)
XLA Ops:
  0.0 0.0 copy-start
  0.0 1.7 %copy-done = bf16[1,1,12,3,2,128,128]{6,5,4,3,2,1,0:T(8,128)(2,1)S(1)} copy-done((bf16[1,1,12,3,2,128,128]{6,5,4,3,2,1,0:T(8,128)(2,1)S(1)}, bf16[1,1,12,3,2,128,128]{6,5,4,3,2,1,0:T(8,128)(2,1)}, u32[]{:S(2)}) %copy-start) | copy-done | bytes 2359320
  1.7 0.0 copy-start.1
  1.7 1.1 %copy-done.1 = bf16[1,1,12,2,128,128]{5,4,3,2,1,0:T(8,128)(2,1)S(1)} copy-done((bf16[1,1,12,2,128,128]{5,4,3,2,1,0:T(8,128)(2,1)S(1)}, bf16[1,1,12,2,128,128]{5,4,3,2,1,0:T(8,128)(2,1)}, u32[]{:S(2)}) %copy-start.1) | copy-done | bytes 786456
  2.8 0.0 copy-start.2
  2.8 0.9 %copy-done.2 = bf16[4,128,128]{2,1,0:T(8,128)(2,1)S(1)} copy-done((bf16[4,128,128]{2,1,0:T(8,128)(2,1)S(1)}, bf16[4,128,128]{2,1,0:T(8,128)(2,1)}, u32[]{:S(2)}) %copy-start.2) | copy-done | bytes 131096
  3.7 0.0 copy-start.3
  3.7 0.7 %copy-done.3 = s32[12]{0:T(128)S(1)} copy-done((s32[12]{0:T(128)S(1)}, s32[12]{0:T(128)}, u32[]{:S(2)}) %copy-start.3) | copy-done | bytes 72
  4.4 0.0 copy-start.4
  4.4 0.7 %copy-done.4 = s32[1,3]{1,0:T(1,128)S(1)} copy-done((s32[1,3]{1,0:T(1,128)S(1)}, s32[1,3]{1,0:T(1,128)}, u32[]{:S(2)}) %copy-start.4) | copy-done | bytes 36
  5.0 0.0 copy-start.5
  5.0 0.7 %copy-done.5 = s32[32]{0:T(128)S(1)} copy-done((s32[32]{0:T(128)S(1)}, s32[32]{0:T(128)}, u32[]{:S(2)}) %copy-start.5) | copy-done | bytes 152
  5.7 0.0 copy-start.6
  5.7 0.7 %copy-done.6 = f32[32]{0:T(128)S(1)} copy-done((f32[32]{0:T(128)S(1)}, f32[32]{0:T(128)}, u32[]{:S(2)}) %copy-start.6) | copy-done | bytes 152
  6.3 46.1 %shard_map.73 = bf16[8,1,2,192,128]{4,3,2,1,0:T(8,128)(2,1)S(1)} custom-call(bf16[1,1,12,3,2,128,128]{6,5,4,3,2,1,0:T(8,128)(2,1)S(1)} %copy-done, bf16[1,1,12,2,128,128]{5,4,3,2,1,0:T(8,128)(2,1)S(1)} %copy-done.1, bf16[4,128,128]{2,1,0:T(8,128)(2,1)S(1)} %copy-done.2, s32[12]{0:T(128)S(1)} %copy-done.3, s32[1,3]{1,0:T(1,128)S(1)} %copy-done.4, ...), custom_call_target="tpu_custom_call" | custom-call | flops 1509949440 | bytes 3145728 | tf_op jit(solution)/shard_map/pallas_call | solution.py:224
  52.4 0.9 %copy.9 = bf16[8,1,2,192,128]{4,3,2,1,0:T(8,128)(2,1)} copy(bf16[8,1,2,192,128]{4,3,2,1,0:T(8,128)(2,1)S(1)} %shard_map.73) | data formatting | bytes 1572864
Async XLA Ops:
  0.0 1.7 %copy-start = (bf16[1,1,12,3,2,128,128]{6,5,4,3,2,1,0:T(8,128)(2,1)S(1)}, bf16[1,1,12,3,2,128,128]{6,5,4,3,2,1,0:T(8,128)(2,1)}, u32[]{:S(2)}) copy-start(bf16[1,1,12,3,2,128,128]{6,5,4,3,2,1,0:T(8,128)(2,1)} %green.1) | copy-start | bytes 7077892
  1.7 1.1 %copy-start.1 = (bf16[1,1,12,2,128,128]{5,4,3,2,1,0:T(8,128)(2,1)S(1)}, bf16[1,1,12,2,128,128]{5,4,3,2,1,0:T(8,128)(2,1)}, u32[]{:S(2)}) copy-start(bf16[1,1,12,2,128,128]{5,4,3,2,1,0:T(8,128)(2,1)} %sigma.1) | copy-start | bytes 2359300
  2.8 0.9 %copy-start.2 = (bf16[4,128,128]{2,1,0:T(8,128)(2,1)S(1)}, bf16[4,128,128]{2,1,0:T(8,128)(2,1)}, u32[]{:S(2)}) copy-start(bf16[4,128,128]{2,1,0:T(8,128)(2,1)} %coupling.1) | copy-start | bytes 393220
  3.7 0.7 %copy-start.3 = (s32[12]{0:T(128)S(1)}, s32[12]{0:T(128)}, u32[]{:S(2)}) copy-start(s32[12]{0:T(128)} %pattern.1) | copy-start | bytes 148
  4.4 0.7 %copy-start.4 = (s32[1,3]{1,0:T(1,128)S(1)}, s32[1,3]{1,0:T(1,128)}, u32[]{:S(2)}) copy-start(s32[1,3]{1,0:T(1,128)} %neighbours.1) | copy-start | bytes 40
  5.0 0.7 %copy-start.5 = (s32[32]{0:T(128)S(1)}, s32[32]{0:T(128)}, u32[]{:S(2)}) copy-start(s32[32]{0:T(128)} %offsets.1) | copy-start | bytes 388
  5.7 0.7 %copy-start.6 = (f32[32]{0:T(128)S(1)}, f32[32]{0:T(128)}, u32[]{:S(2)}) copy-start(f32[32]{0:T(128)} %tap_weight.1) | copy-start | bytes 388

commit v2 on v1

--- a/solution.py
+++ b/solution.py
@@ -16,12 +16,17 @@
     momenta,
     green,
     sigma,
+    coupling_in,
+    pattern_in,
+    neighbours_in,
+    offsets_in,
+    tap_weight_in,
+    out,
     coupling,
     pattern,
     neighbours,
     offsets,
     tap_weight,
-    out,
     gbuf,
     sbuf,
     lesser,
@@ -29,6 +34,7 @@
     mixed,
     gathered,
     table,
+    small_sem,
     gsem,
     ssem,
     zsend,
@@ -46,12 +52,32 @@
     above = lax.rem(mom + 1, momenta)
     below = lax.rem(mom + momenta - 1, momenta)
 
-    group = me // 2
     span = max(1, 2 * own_rows // orb)
-    start = lax.rem(group * (2 * own_rows) // orb + span, slabs)
+    span = span if slabs % span == 0 else 1
+    inner = sorted(range(span), key=lambda place: -abs(2 * place - span + 1))
+
+    def start_of(device):
+        return ((device // 2) * (2 * own_rows) // orb + span) % slabs
+
+    start = lax.rem((me // 2) * (2 * own_rows) // orb + span, slabs)
 
     def slab_at(step):
-        return lax.rem(start + step, slabs)
+        inside = lax.rem(step, span)
+        moved = sum(jnp.where(inside == i, inner[i], 0) for i in range(span))
+        return lax.rem(start + step - inside + moved, slabs)
+
+    def place_of(device, turn):
+        return turn if device % 2 == 0 else per_owner - 1 - turn
+
+    step_of = [i - i % span + inner.index(i % span) for i in range(slabs)]
+    last_step = []
+    for turn in range(per_owner):
+        latest = 0
+        for owner in range(energies):
+            piece = owner * per_owner + place_of(owner, turn)
+            for source in range(energies):
+                latest = max(latest, step_of[(piece // per_slab - start_of(source)) % slabs])
+        last_step.append(latest)
 
     barrier = pltpu.get_barrier_semaphore()
     for to in (above, below):
@@ -70,8 +96,25 @@
     def _(step):
         green_copy(slab_at(step)).start()
 
+    small = [
+        pltpu.make_async_copy(source, target, small_sem.at[i])
+        for i, (source, target) in enumerate(
+            [
+                (coupling_in, coupling),
+                (pattern_in, pattern),
+                (neighbours_in, neighbours),
+                (offsets_in, offsets),
+                (tap_weight_in, tap_weight),
+            ]
+        )
+    ]
+    for copy in small:
+        copy.start()
+
     sbuf[0] = jnp.zeros(sbuf.shape[1:], sbuf.dtype)
     sbuf[slabs + 1] = jnp.zeros(sbuf.shape[1:], sbuf.dtype)
+    for copy in small:
+        copy.wait()
     sigma_copy.wait()
 
     def halo_copy(slab, side, to):
@@ -149,8 +192,7 @@
             device_id_type=MESH,
         )
 
-    @pl.loop(0, slabs)
-    def _(step):
+    def mix(step):
         slab = slab_at(step)
         halo_copy(slab, 0, above).wait_recv()
         halo_copy(slab, 1, below).wait_recv()
@@ -173,13 +215,14 @@
                 mixed[slab, :, rows, :] = value
                 mixed_copy(slab, part, owner, me, place).start()
 
-    for place in range(per_owner):
+    block = 16
+    blocks = unit // block
+
+    def band(turn):
+        place = jnp.where(lax.rem(me, 2) == 0, turn, per_owner - 1 - turn)
         for step in range(1, energies):
             source = lax.rem(me + step, energies)
             mixed_copy(0, 0, source, source, place).wait_recv()
-
-        block = 16
-        blocks = unit // block
 
         @pl.loop(0, 2 * blocks)
         def _(index):
@@ -195,6 +238,16 @@
                     total = term if total is None else total + term
                 out[e, 0, part, rows, :] = total.astype(jnp.bfloat16)
 
+    done = 0
+    for turn in range(per_owner):
+        upto = max(done, last_step[turn] + 1)
+        if upto > done:
+            pl.loop(done, upto)(mix)
+        done = upto
+        band(turn)
+    if done < slabs:
+        pl.loop(done, slabs)(mix)
+
     @pl.loop(0, slabs)
     def _(slab):
         halo_copy(slab, 0, above).wait_send()
@@ -216,17 +269,21 @@
     own_rows = slabs * orb // energies
     unit = math.gcd(orb, own_rows)
     table_rows = -(-(2 * energies - 1) // 8) * 8
-    any_space = pl.BlockSpec(memory_space=pl.ANY)
+    hbm = pl.BlockSpec(memory_space=pltpu.HBM)
     vmem = pl.BlockSpec(memory_space=pltpu.VMEM)
-    smem = pl.BlockSpec(memory_space=pltpu.SMEM)
     bf16 = jnp.bfloat16
     products = 30 * slabs * orb**3
     return pl.pallas_call(
         functools.partial(kernel, energies, momenta),
-        out_shape=jax.ShapeDtypeStruct((energies, 1, 2, own_rows, orb), bf16),
-        in_specs=[any_space, any_space, vmem, smem, smem, smem, smem],
+        out_shape=pltpu.VMEM((energies, 1, 2, own_rows, orb), bf16),
+        in_specs=[hbm] * 7,
         out_specs=vmem,
         scratch_shapes=[
+            pltpu.VMEM(coupling.shape, bf16),
+            pltpu.SMEM(pattern.shape, jnp.int32),
+            pltpu.SMEM(neighbours.shape, jnp.int32),
+            pltpu.SMEM(offsets.shape, jnp.int32),
+            pltpu.SMEM(tap_weight.shape, jnp.float32),
             pltpu.VMEM((slabs, 3, 2, orb, orb), bf16),
             pltpu.VMEM((slabs + 2, 2, orb, orb), bf16),
             pltpu.VMEM((slabs, 2, orb, orb), bf16),
@@ -234,6 +291,7 @@
             pltpu.VMEM((slabs, 2, orb, orb), bf16),
             pltpu.VMEM((energies, 2, own_rows, orb), bf16),
             pltpu.VMEM((table_rows, orb), jnp.float32),
+            pltpu.SemaphoreType.DMA((5,)),
             pltpu.SemaphoreType.DMA((slabs,)),
             pltpu.SemaphoreType.DMA,
             pltpu.SemaphoreType.DMA((2, slabs)),
@@ -242,12 +300,12 @@
             pltpu.SemaphoreType.DMA((energies, own_rows // unit)),
         ],
         compiler_params=pltpu.CompilerParams(
-            collective_id=0, has_side_effects=True, vmem_limit_bytes=32 * 1024 * 1024
+            collective_id=0, has_side_effects=True, vmem_limit_bytes=40 * 1024 * 1024
         ),
         cost_estimate=pl.CostEstimate(
             flops=2 * products, bytes_accessed=8 * slabs * orb * orb * 2, transcendentals=0
         ),
-    )(green_ret, sigma_in, coupling, pattern, neighbours, offsets, tap_weight)
+    )(*[pltpu.with_memory_space_constraint(x, pltpu.HBM) for x in (green_ret, sigma_in, coupling, pattern, neighbours, offsets, tap_weight)])
 
 
 def solution(mesh):

time: 53.8 us -> 45.1 us (0.84)
  local copies, waits for them, and re-layouts: 7.2 us -> 0.88 us
  Pallas kernels: 46.1 us -> 43.6 us
    unnamed x15 -> x1, local copies, waits for them, and re-layouts: 7.2 us -> 0.88 us
    pallas_call x1, Pallas kernels: 46.1 us -> 43.6 us  [shards(): pl.pallas_call(functools.partial(kernel, energies, momenta), out_shape=pl...]
where the time goes in v2:
time: 45.1 us; the launch traced here: 44.5 us
  Pallas kernels  43.6 us (97%)
  local copies, waits for them, and re-layouts  0.88 us (2%)
    pallas_call x1, Pallas kernels, shards(): pl.pallas_call(functools.partial(kernel, energies, momenta), out_shape=pl...  43.6 us

profile of v2, /device:TPU:0, one launch (start us, length us, event | category | flops | bytes accessed | tf_op | source)
XLA Modules:
  0.0 44.5 jit_solution(2065690671184396039)
XLA Ops:
  0.0 43.6 %shard_map.73 = bf16[8,1,2,192,128]{4,3,2,1,0:T(8,128)(2,1)S(1)} custom-call(bf16[1,1,12,3,2,128,128]{6,5,4,3,2,1,0:T(8,128)(2,1)} %green.1, bf16[1,1,12,2,128,128]{5,4,3,2,1,0:T(8,128)(2,1)} %sigma.1, bf16[4,128,128]{2,1,0:T(8,128)(2,1)} %coupling_in.1, s32[12]{0:T(128)} %pattern_in.1, s32[1,3]{1,0:T(1,128)} %neighbours_in.1, s32[32]{0:T(128)} %offsets_in.1, ...), custom_call_target="tpu_custom_call" | custom-call | flops 1509949440 | bytes 3145728 | tf_op jit(solution)/shard_map/pallas_call | solution.py:276
  43.7 0.9 %copy.9 = bf16[8,1,2,192,128]{4,3,2,1,0:T(8,128)(2,1)} copy(bf16[8,1,2,192,128]{4,3,2,1,0:T(8,128)(2,1)S(1)} %shard_map.73) | data formatting | bytes 1572864

commit v3 on v2

--- a/solution.py
+++ b/solution.py
@@ -31,6 +31,7 @@
     sbuf,
     lesser,
     halo,
+    relay,
     mixed,
     gathered,
     table,
@@ -39,6 +40,8 @@
     ssem,
     zsend,
     zrecv,
+    rsend,
+    rrecv,
     asend,
     arecv,
 ):
@@ -56,45 +59,12 @@
     span = span if slabs % span == 0 else 1
     inner = sorted(range(span), key=lambda place: -abs(2 * place - span + 1))
 
-    def start_of(device):
-        return ((device // 2) * (2 * own_rows) // orb + span) % slabs
-
     start = lax.rem((me // 2) * (2 * own_rows) // orb + span, slabs)
 
     def slab_at(step):
         inside = lax.rem(step, span)
         moved = sum(jnp.where(inside == i, inner[i], 0) for i in range(span))
         return lax.rem(start + step - inside + moved, slabs)
-
-    def place_of(device, turn):
-        return turn if device % 2 == 0 else per_owner - 1 - turn
-
-    step_of = [i - i % span + inner.index(i % span) for i in range(slabs)]
-    last_step = []
-    for turn in range(per_owner):
-        latest = 0
-        for owner in range(energies):
-            piece = owner * per_owner + place_of(owner, turn)
-            for source in range(energies):
-                latest = max(latest, step_of[(piece // per_slab - start_of(source)) % slabs])
-        last_step.append(latest)
-
-    barrier = pltpu.get_barrier_semaphore()
-    for to in (above, below):
-        pl.semaphore_signal(barrier, inc=1, device_id={"mom": to}, device_id_type=MESH)
-    for step in range(1, energies):
-        to = lax.rem(me + step, energies)
-        pl.semaphore_signal(barrier, inc=1, device_id={"energy": to}, device_id_type=MESH)
-
-    sigma_copy = pltpu.make_async_copy(sigma.at[0, 0], sbuf.at[pl.ds(1, slabs)], ssem)
-    sigma_copy.start()
-
-    def green_copy(slab):
-        return pltpu.make_async_copy(green.at[0, 0, slab], gbuf.at[slab], gsem.at[slab])
-
-    @pl.loop(0, slabs)
-    def _(step):
-        green_copy(slab_at(step)).start()
 
     small = [
         pltpu.make_async_copy(source, target, small_sem.at[i])
@@ -111,6 +81,23 @@
     for copy in small:
         copy.start()
 
+    barrier = pltpu.get_barrier_semaphore()
+    for to in (above, below):
+        pl.semaphore_signal(barrier, inc=1, device_id={"mom": to}, device_id_type=MESH)
+    for step in range(1, energies):
+        to = lax.rem(me + step, energies)
+        pl.semaphore_signal(barrier, inc=1, device_id={"energy": to}, device_id_type=MESH)
+
+    sigma_copy = pltpu.make_async_copy(sigma.at[0, 0], sbuf.at[pl.ds(1, slabs)], ssem)
+    sigma_copy.start()
+
+    def green_copy(slab):
+        return pltpu.make_async_copy(green.at[0, 0, slab], gbuf.at[slab], gsem.at[slab])
+
+    @pl.loop(0, slabs)
+    def _(step):
+        green_copy(slab_at(step)).start()
+
     sbuf[0] = jnp.zeros(sbuf.shape[1:], sbuf.dtype)
     sbuf[slabs + 1] = jnp.zeros(sbuf.shape[1:], sbuf.dtype)
     for copy in small:
@@ -128,11 +115,41 @@
         )
 
     low = (mom < momenta // 2).astype(jnp.int32)
-    first_to = jnp.where(low == 1, below, above)
-    second_to = jnp.where(low == 1, above, below)
-
-    @pl.loop(0, slabs)
-    def _(step):
+    outward = jnp.where(low == 1, below, above)
+    inward = jnp.where(low == 1, above, below)
+
+    line = momenta == 4
+    inside = (mom == 1) | (mom == 2)
+
+    def to_inward(step):
+        return halo_copy(slab_at(step), 1 - low, inward)
+
+    def to_outward(step):
+        return halo_copy(slab_at(step), low, outward)
+
+    def relay_in(step):
+        slab = slab_at(step)
+        return pltpu.make_async_remote_copy(
+            src_ref=halo.at[1 - low, slab],
+            dst_ref=relay.at[slab],
+            send_sem=rsend.at[0, slab],
+            recv_sem=rrecv.at[slab],
+            device_id={"mom": inward},
+            device_id_type=MESH,
+        )
+
+    def relay_out(step):
+        slab = slab_at(step)
+        return pltpu.make_async_remote_copy(
+            src_ref=relay.at[slab],
+            dst_ref=halo.at[1 - low, slab],
+            send_sem=rsend.at[1, slab],
+            recv_sem=zrecv.at[1 - low, slab],
+            device_id={"mom": outward},
+            device_id_type=MESH,
+        )
+
+    def compute(step):
         slab = slab_at(step)
         green_copy(slab).wait()
         couple = coupling[pattern[slab]]
@@ -165,9 +182,6 @@
         def _():
             pl.semaphore_wait(barrier, energies + 1)
 
-        halo_copy(slab, low, first_to).start()
-        halo_copy(slab, 1 - low, second_to).start()
-
     shift = lax.broadcasted_iota(jnp.int32, table.shape, 0) - (energies - 1)
     summed = jnp.zeros(table.shape, jnp.float32)
     for tap in range(offsets.shape[0]):
@@ -194,8 +208,15 @@
 
     def mix(step):
         slab = slab_at(step)
-        halo_copy(slab, 0, above).wait_recv()
-        halo_copy(slab, 1, below).wait_recv()
+        if line:
+            halo_copy(slab, low, outward).wait_recv()
+
+            @pl.when(jnp.logical_not(inside))
+            def _():
+                halo_copy(slab, 1 - low, inward).wait_recv()
+        else:
+            halo_copy(slab, 0, above).wait_recv()
+            halo_copy(slab, 1, below).wait_recv()
         for part in range(per_slab):
             rows = pl.ds(part * unit, unit)
             value = weights[0] * halo[0, slab, :, rows, :].astype(jnp.float32)
@@ -238,20 +259,74 @@
                     total = term if total is None else total + term
                 out[e, 0, part, rows, :] = total.astype(jnp.bfloat16)
 
-    done = 0
+    if line:
+        ahead = min(2, slabs)
+        lag = ahead + 3
+
+        @pl.loop(0, slabs + lag)
+        def _(tick):
+            @pl.when(tick < slabs)
+            def _():
+                compute(tick)
+
+                @pl.when(inside)
+                def _():
+                    to_outward(tick).start()
+
+                @pl.when(jnp.logical_not(inside) | (tick < ahead))
+                def _():
+                    to_inward(tick).start()
+
+            @pl.when(inside & (tick >= ahead) & (tick < slabs + ahead))
+            def _():
+                step = tick - ahead
+                to_inward(step).wait_recv()
+                relay_in(step).start()
+
+                @pl.when(lax.rem(step, 2) == 1)
+                def _():
+                    to_inward(ahead + step // 2).start()
+
+                @pl.when(step == slabs - 1)
+                def _():
+                    @pl.loop(ahead + slabs // 2, slabs)
+                    def _(rest):
+                        to_inward(rest).start()
+
+            @pl.when(inside & (tick >= lag))
+            def _():
+                relay_in(tick - lag).wait_recv()
+                relay_out(tick - lag).start()
+
+            @pl.when((tick > lag) & (lax.rem(tick - lag, 2) == 1))
+            def _():
+                mix((tick - lag) // 2)
+
+    else:
+
+        @pl.loop(0, slabs)
+        def _(step):
+            compute(step)
+            to_outward(step).start()
+            to_inward(step).start()
+
+    done = slabs // 2 if line else 0
+    pl.loop(done, slabs)(mix)
     for turn in range(per_owner):
-        upto = max(done, last_step[turn] + 1)
-        if upto > done:
-            pl.loop(done, upto)(mix)
-        done = upto
         band(turn)
-    if done < slabs:
-        pl.loop(done, slabs)(mix)
 
     @pl.loop(0, slabs)
     def _(slab):
-        halo_copy(slab, 0, above).wait_send()
-        halo_copy(slab, 1, below).wait_send()
+        halo_copy(slab, 1 - low, inward).wait_send()
+        if line:
+
+            @pl.when(inside)
+            def _():
+                halo_copy(slab, low, outward).wait_send()
+                relay_in(slab).wait_send()
+                relay_out(slab).wait_send()
+        else:
+            halo_copy(slab, low, outward).wait_send()
         for part in range(per_slab):
             piece = slab * per_slab + part
             owner = piece // per_owner
@@ -289,6 +364,7 @@
             pltpu.VMEM((slabs, 2, orb, orb), bf16),
             pltpu.VMEM((2, slabs, 2, orb, orb), bf16),
             pltpu.VMEM((slabs, 2, orb, orb), bf16),
+            pltpu.VMEM((slabs, 2, orb, orb), bf16),
             pltpu.VMEM((energies, 2, own_rows, orb), bf16),
             pltpu.VMEM((table_rows, orb), jnp.float32),
             pltpu.SemaphoreType.DMA((5,)),
@@ -296,6 +372,8 @@
             pltpu.SemaphoreType.DMA,
             pltpu.SemaphoreType.DMA((2, slabs)),
             pltpu.SemaphoreType.DMA((2, slabs)),
+            pltpu.SemaphoreType.DMA((2, slabs)),
+            pltpu.SemaphoreType.DMA((slabs,)),
             pltpu.SemaphoreType.DMA((slabs, orb // unit)),
             pltpu.SemaphoreType.DMA((energies, own_rows // unit)),
         ],

time: 45.1 us -> 45 us (level)
  no operation moved by 1% of the time
where the time goes in v3:
time: 45 us; the launch traced here: 44.4 us
  Pallas kernels  43.6 us (97%)
  local copies, waits for them, and re-layouts  0.88 us (2%)
    pallas_call x1, Pallas kernels, shards(): pl.pallas_call(functools.partial(kernel, energies, momenta), out_shape=pl...  43.6 us

profile of v3, /device:TPU:0, one launch (start us, length us, event | category | flops | bytes accessed | tf_op | source)
XLA Modules:
  0.0 44.4 jit_solution(16277100749662389509)
XLA Ops:
  0.0 43.6 %shard_map.73 = bf16[8,1,2,192,128]{4,3,2,1,0:T(8,128)(2,1)S(1)} custom-call(bf16[1,1,12,3,2,128,128]{6,5,4,3,2,1,0:T(8,128)(2,1)} %green.1, bf16[1,1,12,2,128,128]{5,4,3,2,1,0:T(8,128)(2,1)} %sigma.1, bf16[4,128,128]{2,1,0:T(8,128)(2,1)} %coupling_in.1, s32[12]{0:T(128)} %pattern_in.1, s32[1,3]{1,0:T(1,128)} %neighbours_in.1, s32[32]{0:T(128)} %offsets_in.1, ...), custom_call_target="tpu_custom_call" | custom-call | flops 1509949440 | bytes 3145728 | tf_op jit(solution)/shard_map/pallas_call | solution.py:351
  43.6 0.9 %copy.9 = bf16[8,1,2,192,128]{4,3,2,1,0:T(8,128)(2,1)} copy(bf16[8,1,2,192,128]{4,3,2,1,0:T(8,128)(2,1)S(1)} %shard_map.73) | data formatting | bytes 1572864
